TPU v7x, 32 devices: a whole 2x2x4 slice. The times are simulated.
32 devices in a mesh: groups: 2 (over x), tiles: 16 (over z, y, core).
Axes of the slice: x: 2, y: 2, z: 4, core: 2. Of those that a mesh axis runs over, the one named last changes fastest.
Arguments:
- video_q: bfloat16 [8192, 3072], P(('groups', 'tiles')), parts along dimension 0, may hold values from -88 to 88, as said below
- video_k: bfloat16 [8192, 3072], P(('groups', 'tiles')), parts along dimension 0, may hold values from -4 to 4, as said below
- video_v: bfloat16 [8192, 3072], P(('groups', 'tiles')), parts along dimension 0, may hold values from -5 to 5
- text_q: bfloat16 [512, 3072], P('groups'), parts along dimension 0, may hold values from -88 to 88
- text_k: bfloat16 [512, 3072], P('groups'), parts along dimension 0, may hold values from -5 to 5
- text_v: bfloat16 [512, 3072], P('groups'), parts along dimension 0, may hold values from -5 to 5
- window: int32 [32, 6], P('tiles'), may hold values from 0 to 13, as said below
- counts: int32 [64], P(('groups', 'tiles')), parts along dimension 0, may hold values from 1 to 128, as said below
- text_count: int32 [2], P('groups'), parts along dimension 0, may hold values from 64 to 256
Outputs:
- video_out: bfloat16 [8192, 3072], P(('groups', 'tiles')), parts along dimension 0
- text_out: bfloat16 [512, 3072], P(('groups', 'tiles')), parts along dimension 0
There are 2 independent parts, one for each index of `groups`. A program takes and returns all parts, laid end to end along the dimension named above; an argument that names none is the same for every part. Nothing has to cross between parts.
Inputs may be any that keep to these rules, and one draw needn't show every extreme that they name: `video_q`: queries drawn for the problem. `video_k`: keys drawn for the problem. `window`: each row names 6 different codes, among them always 3, 6, 9 and 12. `counts`: valid tokens are the first slots of a tile.
All inputs are finite; a program needn't handle non-finite values.
Results may differ from a plain program's by a relative error of at most 0.003.
Values may be sent and summed in bfloat16 or wider, within the bound.
A program may use at most 192 MiB of HBM per device.

v0:
```python
import math

import jax
import jax.numpy as jnp
from jax import lax
from jax.sharding import PartitionSpec as P

HEADS = 24
HD = 128
NR = 4
TEXT = 256


def passed_along(x, axis, by):
    length = lax.axis_size(axis)
    return lax.ppermute(x, axis, [(i, (i + by) % length) for i in range(length)])


def per_device(video_q, video_k, video_v, text_q, text_k, text_v, window, counts, text_count):
    columns = counts.shape[0]
    tok_tile = video_q.shape[0] // columns
    model_width = video_q.shape[1]
    score_scale = 1.0 / math.sqrt(HD)
    group_size = lax.axis_size("tiles")
    position = lax.axis_index("tiles")
    spot = (position + group_size // 2 + NR + NR // 2) % group_size
    row_pos = spot % NR
    time_pos = spot // NR
    last_time = group_size // NR - 1
    keys_own = video_k.reshape(columns, tok_tile, model_width)
    values_own = video_v.reshape(columns, tok_tile, model_width)
    earlier_side = passed_along((keys_own, values_own, counts), "tiles", NR)
    later_side = passed_along((keys_own, values_own, counts), "tiles", -NR)
    above_side = passed_along((keys_own, values_own, counts), "tiles", 1)
    below_side = passed_along((keys_own, values_own, counts), "tiles", -1)
    earlier_count = jnp.where(time_pos == 0, 0, earlier_side[2])
    later_count = jnp.where(time_pos == last_time, 0, later_side[2])
    above_count = jnp.where(row_pos == 0, 0, above_side[2])
    below_count = jnp.where(row_pos == NR - 1, 0, below_side[2])
    column_pad = ((0, 0), (1, 1), (0, 0), (0, 0))
    key_flat = jnp.pad(
        jnp.stack([keys_own, earlier_side[0], later_side[0], above_side[0], below_side[0]]),
        column_pad,
    )
    key_flat = key_flat.reshape(5 * (columns + 2), tok_tile, model_width)
    value_flat = jnp.pad(
        jnp.stack([values_own, earlier_side[1], later_side[1], above_side[1], below_side[1]]),
        column_pad,
    )
    value_flat = value_flat.reshape(5 * (columns + 2), tok_tile, model_width)
    count_flat = jnp.pad(
        jnp.stack([counts, earlier_count, later_count, above_count, below_count]), ((0, 0), (1, 1))
    ).reshape(-1)
    cell_codes = jnp.concatenate(
        [jnp.ones((columns, 1), jnp.int32), window + (window >= 1)], axis=1
    )
    flat_index = (
        cell_codes // 3 * (columns + 2)
        + jnp.arange(columns, dtype=jnp.int32)[:, None]
        + cell_codes % 3
    )
    slot_ids = jnp.arange(tok_tile, dtype=jnp.int32)
    text_valid = jnp.arange(TEXT, dtype=jnp.int32) < text_count[0]
    text_keys = text_k.reshape(TEXT, HEADS, HD)
    text_values = text_v.reshape(TEXT, HEADS, HD)
    query_tiles = video_q.reshape(columns, tok_tile, HEADS, HD)

    def one_tile(tile_items):
        q_tile, flat_row, q_count = tile_items
        keys_chosen = key_flat[flat_row].reshape(-1, HEADS, HD)
        values_chosen = value_flat[flat_row].reshape(-1, HEADS, HD)
        key_valid = (slot_ids[None, :] < count_flat[flat_row][:, None]).reshape(-1)
        video_scores = (
            jnp.einsum("qhd,khd->hqk", q_tile, keys_chosen, preferred_element_type=jnp.float32)
            * score_scale
        )
        video_scores = jnp.where(key_valid[None, None, :], video_scores, -jnp.inf)
        text_scores = (
            jnp.einsum("qhd,khd->hqk", q_tile, text_keys, preferred_element_type=jnp.float32)
            * score_scale
        )
        text_scores = jnp.where(text_valid[None, None, :], text_scores, -jnp.inf)
        row_top = jnp.maximum(jnp.max(video_scores, axis=-1), jnp.max(text_scores, axis=-1))[
            ..., None
        ]
        video_probs = jnp.exp(video_scores - row_top)
        text_probs = jnp.exp(text_scores - row_top)
        denom = jnp.sum(video_probs, axis=-1) + jnp.sum(text_probs, axis=-1)
        numer = jnp.einsum(
            "hqk,khd->qhd",
            video_probs.astype(jnp.bfloat16),
            values_chosen,
            preferred_element_type=jnp.float32,
        )
        numer = numer + jnp.einsum(
            "hqk,khd->qhd",
            text_probs.astype(jnp.bfloat16),
            text_values,
            preferred_element_type=jnp.float32,
        )
        result = numer / denom.T[:, :, None]
        query_valid = slot_ids < q_count
        return jnp.where(query_valid[:, None, None], result, 0.0).astype(jnp.bfloat16)

    video_out = lax.map(one_tile, (query_tiles, flat_index, counts)).reshape(
        columns * tok_tile, model_width
    )
    key_heads = video_k.reshape(columns * tok_tile, HEADS, HD)
    value_heads = video_v.reshape(columns * tok_tile, HEADS, HD)
    local_valid = (slot_ids[None, :] < counts[:, None]).reshape(-1)
    text_queries = text_q.reshape(TEXT, HEADS, HD)
    global_scores = (
        jnp.einsum("qhd,khd->hqk", text_queries, key_heads, preferred_element_type=jnp.float32)
        * score_scale
    )
    global_scores = jnp.where(local_valid[None, None, :], global_scores, -jnp.inf)
    local_top = jnp.max(global_scores, axis=-1)
    global_top = lax.pmax(local_top, "tiles")
    weights = jnp.exp(global_scores - global_top[..., None])
    denom_part = jnp.sum(weights, axis=-1).T
    numer_part = jnp.einsum(
        "hqk,khd->qhd",
        weights.astype(jnp.bfloat16),
        value_heads,
        preferred_element_type=jnp.float32,
    )
    numer_part = numer_part.reshape(TEXT, model_width)
    share_rows = TEXT // group_size
    numer_rows, denom_rows = (
        lax.psum_scatter(numer_part, "tiles", scatter_dimension=0, tiled=True),
        lax.psum_scatter(denom_part, "tiles", scatter_dimension=0, tiled=True),
    )
    text_result = numer_rows.reshape(share_rows, HEADS, HD) / denom_rows[:, :, None]
    row_ids = position * share_rows + jnp.arange(share_rows, dtype=jnp.int32)
    text_out = jnp.where((row_ids < text_count[0])[:, None, None], text_result, 0.0)
    text_out = text_out.astype(jnp.bfloat16).reshape(share_rows, model_width)
    return (video_out, text_out)


def solution(mesh):
    return jax.shard_map(
        per_device,
        mesh=mesh,
        in_specs=(
            P(("groups", "tiles"), None),
            P(("groups", "tiles"), None),
            P(("groups", "tiles"), None),
            P("groups", None),
            P("groups", None),
            P("groups", None),
            P("tiles", None),
            P(("groups", "tiles")),
            P("groups"),
        ),
        out_specs=(P(("groups", "tiles"), None), P(("groups", "tiles"), None)),
        check_vma=False,
    )
```

profile of v0, /device:TPU:8, one launch (start us, length us, event | category | flops | bytes accessed | tf_op | source)
XLA Modules:
  0.0 408.5 jit_solution(15297029560444386600)
XLA Ops:
  7.3 2.6 collective-permute-start.7
  9.9 1.6 collective-permute-start.4
  11.9 1.6 collective-permute-start.8
  13.5 0.7 compare_bitcast_fusion
  14.3 5.2 %fusion.45 = (f32[24,256]{1,0:T(8,128)S(1)}, f32[24,256,256]{1,2,0:T(8,128)}) fusion(pred[256]{0:T(512)(128)(4,1)S(1)} %compare_bitcast_fusion, bf16[256,3072]{1,0:T(8,128)(2,1)} %param.12, bf16[256,3072]{1,0:T(8,128)(2,1)S(1)} %copy-done), kind=kOutput, calls=%fused_computation.53 | convolution fusion | flops 407365632 | bytes 9462016 | tf_op jit(solution)/shard_map/qhd,khd->hqk/dot_general | solution.py:113
  19.4 74.3 %pmax.7 = f32[24,256]{1,0:T(8,128)S(1)} all-reduce(f32[24,256]{1,0:T(8,128)S(1)} %get-tuple-element.181), channel_id=1, replica_groups=mesh['groups'=2,'tiles'=16] {'tiles'}, use_global_device_ids=true, to_apply=%region_7.8 | all-reduce | flops 6144 | bytes 49152 | tf_op jit(solution)/shard_map/pmax | solution.py:118
  93.7 4.1 %fusion.46 = f32[24,256]{1,0:T(8,128)S(1)} fusion(f32[24,256,256]{1,2,0:T(8,128)} %get-tuple-element.182, f32[24,256]{1,0:T(8,128)S(1)} %pmax.7, pred[256]{0:T(512)(128)(4,1)S(1)} %compare_bitcast_fusion), kind=kLoop, calls=%fused_computation.54 | loop fusion | flops 6285312 | bytes 6340864 | tf_op jit(solution)/shard_map/reduce_sum | solution.py:120
  97.8 0.8 copy.79
  98.6 1.7 copy.78
  100.4 6.1 %fusion.48 = f32[24,256,128]{1,2,0:T(8,128)} fusion(bf16[256,24,128]{0,2,1:T(8,128)(2,1)S(1)} %bitcast.162, f32[24,256,256]{1,2,0:T(8,128)} %get-tuple-element.182, f32[24,256]{1,0:T(8,128)S(1)} %pmax.7, pred[256]{0:T(512)(128)(4,1)S(1)} %compare_bitcast_fusion), kind=kOutput, calls=%fused_computation.56 | convolution fusion | flops 408944640 | bytes 11034880 | tf_op jit(solution)/shard_map/hqk,khd->qhd/dot_general | solution.py:121
  106.5 3.5 copy.74
  110.7 0.7 copy-done.7
  111.4 0.7 copy.64
  112.1 0.9 copy.67
  113.0 1.7 copy.65
  114.7 1.6 copy.68
  116.3 2.9 copy.91
  120.5 2.6 constant_dynamic-update-slice_fusion.2
  123.1 2.7 constant_dynamic-update-slice_fusion.1
  125.8 8.5 %collective-permute-start.9 = (bf16[2,128,3072]{2,1,0:T(8,128)(2,1)}, bf16[2,128,3072]{2,1,0:T(8,128)(2,1)}, u32[]{:S(2)}, u32[]{:S(2)}) collective-permute-start(bf16[2,128,3072]{2,1,0:T(8,128)(2,1)} %bitcast.13), channel_id=1, source_target_pairs={{0,12},{1,13},{2,14},{3,15},{4,0},{5,1},{6,2},{7,3},{8,4},{9,5},{1... | collective-permute-start | bytes 4718600 | tf_op jit(solution)/shard_map/ppermute | solution.py:16
  134.3 2.6 collective-permute-start.11
  137.7 2.0 collective-permute-start.1
  139.7 2.7 bitcast_dynamic-update-slice_fusion.3
  142.4 33.8 %collective-permute-done.9 = bf16[2,128,3072]{2,1,0:T(8,128)(2,1)} collective-permute-done((bf16[2,128,3072]{2,1,0:T(8,128)(2,1)}, bf16[2,128,3072]{2,1,0:T(8,128)(2,1)}, u32[]{:S(2)}, u32[]{:S(2)}) %collective-permute-start.9) | collective-permute-done | bytes 1572896 | tf_op jit(solution)/shard_map/ppermute | solution.py:16
  176.2 2.8 bitcast_dynamic-update-slice_fusion.2
  179.1 23.8 %collective-permute-done.10 = bf16[2,128,3072]{2,1,0:T(8,128)(2,1)} collective-permute-done((bf16[2,128,3072]{2,1,0:T(8,128)(2,1)}, bf16[2,128,3072]{2,1,0:T(8,128)(2,1)}, u32[]{:S(2)}, u32[]{:S(2)}) %collective-permute-start.10) | collective-permute-done | bytes 1572896 | tf_op jit(solution)/shard_map/ppermute | solution.py:16
  202.8 2.7 bitcast_dynamic-update-slice_fusion.1
  205.5 26.8 %collective-permute-done.11 = bf16[2,128,3072]{2,1,0:T(8,128)(2,1)} collective-permute-done((bf16[2,128,3072]{2,1,0:T(8,128)(2,1)}, bf16[2,128,3072]{2,1,0:T(8,128)(2,1)}, u32[]{:S(2)}, u32[]{:S(2)}) %collective-permute-start.11) | collective-permute-done | bytes 1572896 | tf_op jit(solution)/shard_map/ppermute | solution.py:16
  232.2 2.8 bitcast_dynamic-update-slice_fusion
  235.0 1.6 bitcast_dynamic-update-slice_fusion.7
  236.6 9.1 %pad.14 = bf16[5,4,128,3072]{3,2,1,0:T(8,128)(2,1)} pad(bf16[5,2,128,3072]{3,2,1,0:T(8,128)(2,1)} %bitcast_dynamic-update-slice_fusion, bf16[]{:T(256)} %constant.82.clone.1), padding=0_0x1_1x0_0x0_0 | pad | bytes 23592962 | tf_op jit(solution)/shard_map/jit(_pad)/pad | solution.py:41
  245.7 9.5 %collective-permute-done.1 = bf16[2,128,3072]{2,1,0:T(8,128)(2,1)S(1)} collective-permute-done((bf16[2,128,3072]{2,1,0:T(8,128)(2,1)}, bf16[2,128,3072]{2,1,0:T(8,128)(2,1)S(1)}, u32[]{:S(2)}, u32[]{:S(2)}) %collective-permute-start.1) | collective-permute-done | bytes 1572896 | tf_op jit(solution)/shard_map/ppermute | solution.py:16
  255.3 26.1 %collective-permute-done.2 = bf16[2,128,3072]{2,1,0:T(8,128)(2,1)S(1)} collective-permute-done((bf16[2,128,3072]{2,1,0:T(8,128)(2,1)}, bf16[2,128,3072]{2,1,0:T(8,128)(2,1)S(1)}, u32[]{:S(2)}, u32[]{:S(2)}) %collective-permute-start.2) | collective-permute-done | bytes 1572896 | tf_op jit(solution)/shard_map/ppermute | solution.py:16
  281.6 5.9 %pad.12 = bf16[5,4,128,3072]{3,2,1,0:T(8,128)(2,1)} pad(bf16[5,2,128,3072]{3,2,1,0:T(8,128)(2,1)S(1)} %bitcast_dynamic-update-slice_fusion.4, bf16[]{:T(256)} %constant.82.clone.1), padding=0_0x1_1x0_0x0_0 | pad | bytes 23592962 | tf_op jit(solution)/shard_map/jit(_pad)/pad | solution.py:46
  287.5 108.6 %while.12 = (s32[]{:T(128)}, bf16[2,128,24,128]{3,2,1,0:T(8,128)(2,1)}, s32[2]{0:T(128)S(1)}, s32[2,7]{1,0:T(2,128)S(1)}, bf16[20,128,3072]{2,1,0:T(8,128)(2,1)}...) while((s32[]{:T(128)}, ...), condition=%wide.region_5.6_spmd.clone.clone, body=%wide.region_0.5_spmd.clone.clone.sunk | while | flops 1852436736 | bytes 173995776 | solution.py:105
  288.3 8.9 %gather_fusion.1 = bf16[7,128,3072]{2,1,0:T(8,128)(2,1)} fusion(bf16[20,128,3072]{2,1,0:T(8,128)(2,1)} %get-tuple-element.289, s32[1024]{0:T(1024)S(1)} %pad_clamp_fusion.2), kind=kCustom, calls=%fused_computation.2.clone.clone.1 | custom fusion | bytes 11010076 | tf_op jit(solution)/shard_map/while/body/eval_jaxpr/gather | solution.py:70
  297.2 4.4 %copy.137 = bf16[112,8,24,128]{3,2,1,0:T(8,128)(2,1)S(1)} copy(bf16[112,8,24,128]{3,1,2,0:T(8,128)(2,1)} %bitcast.156) | data formatting | bytes 11010048 | tf_op jit(solution)/shard_map/while
  301.7 2.5 fusion.95
  304.1 0.7 iota_compare_fusion.5
  305.5 2.7 fusion.97
  308.2 1.2 fusion.98
  309.6 2.3 fusion.96
  311.9 8.8 %gather_fusion.2 = bf16[7,128,3072]{2,1,0:T(8,128)(2,1)} fusion(bf16[20,128,3072]{2,1,0:T(8,128)(2,1)} %get-tuple-element.286, s32[1024]{0:T(1024)S(1)} %pad_clamp_fusion.2), kind=kCustom, calls=%fused_computation.clone.clone.1 | custom fusion | bytes 11010076 | tf_op jit(solution)/shard_map/while/body/eval_jaxpr/gather | solution.py:71
  320.7 6.8 %copy.138 = bf16[112,8,24,128]{3,2,1,0:T(8,128)(2,1)} copy(bf16[112,8,24,128]{3,1,2,0:T(8,128)(2,1)} %bitcast.155) | data formatting | bytes 11010048 | tf_op jit(solution)/shard_map/while
  328.1 0.7 iota_compare_fusion.6
  328.8 10.5 %fusion.99 = bf16[1,128,24,128]{1,3,2,0:T(8,128)(2,1)} fusion(f32[24,128,128]{1,2,0:T(8,128)S(1)} %copy-done.4, f32[24,128,896]{2,1,0:T(8,128)} %copy-done.2, f32[24,128]{1,0:T(8,128)S(1)} %max.12, pred[896]{0:T(1024)(128)(4,1)S(1)} %fusion.94, bf16[896,24,128]{2,1,0:T(8,128)(2,1)} %bitcast.157, f32[128,24]{0,1:T(8,128)S(1)} %add_bitcast_fusion.2, ...), kind=kOutput, calls=%fused_computation.32.clone.1 | convolution fusion | flops 717225984 | bytes 18899968 | tf_op jit(solution)/shard_map/while/body/eval_jaxpr/hqk,khd->qhd/dot_general | solution.py:89
  339.4 1.5 copy.139
  340.9 1.0 constant_dynamic-update-slice_fusion.4
  342.7 8.8 %gather_fusion.1 = bf16[7,128,3072]{2,1,0:T(8,128)(2,1)} fusion(bf16[20,128,3072]{2,1,0:T(8,128)(2,1)} %get-tuple-element.289, s32[1024]{0:T(1024)S(1)} %pad_clamp_fusion.2), kind=kCustom, calls=%fused_computation.2.clone.clone.1 | custom fusion | bytes 11010076 | tf_op jit(solution)/shard_map/while/body/eval_jaxpr/gather | solution.py:70
  351.5 4.3 %copy.137 = bf16[112,8,24,128]{3,2,1,0:T(8,128)(2,1)S(1)} copy(bf16[112,8,24,128]{3,1,2,0:T(8,128)(2,1)} %bitcast.156) | data formatting | bytes 11010048 | tf_op jit(solution)/shard_map/while
  355.9 2.5 fusion.95
  358.4 0.7 iota_compare_fusion.5
  359.8 2.7 fusion.97
  362.5 1.2 fusion.98
  363.9 2.3 fusion.96
  366.2 8.8 %gather_fusion.2 = bf16[7,128,3072]{2,1,0:T(8,128)(2,1)} fusion(bf16[20,128,3072]{2,1,0:T(8,128)(2,1)} %get-tuple-element.286, s32[1024]{0:T(1024)S(1)} %pad_clamp_fusion.2), kind=kCustom, calls=%fused_computation.clone.clone.1 | custom fusion | bytes 11010076 | tf_op jit(solution)/shard_map/while/body/eval_jaxpr/gather | solution.py:71
  375.0 6.8 %copy.138 = bf16[112,8,24,128]{3,2,1,0:T(8,128)(2,1)} copy(bf16[112,8,24,128]{3,1,2,0:T(8,128)(2,1)} %bitcast.155) | data formatting | bytes 11010048 | tf_op jit(solution)/shard_map/while
  382.4 0.7 iota_compare_fusion.6
  383.1 10.5 %fusion.99 = bf16[1,128,24,128]{1,3,2,0:T(8,128)(2,1)} fusion(f32[24,128,128]{1,2,0:T(8,128)S(1)} %copy-done.4, f32[24,128,896]{2,1,0:T(8,128)} %copy-done.2, f32[24,128]{1,0:T(8,128)S(1)} %max.12, pred[896]{0:T(1024)(128)(4,1)S(1)} %fusion.94, bf16[896,24,128]{2,1,0:T(8,128)(2,1)} %bitcast.157, f32[128,24]{0,1:T(8,128)S(1)} %add_bitcast_fusion.2, ...), kind=kOutput, calls=%fused_computation.32.clone.1 | convolution fusion | flops 717225984 | bytes 18899968 | tf_op jit(solution)/shard_map/while/body/eval_jaxpr/hqk,khd->qhd/dot_general | solution.py:89
  393.7 1.5 copy.139
  395.2 1.0 constant_dynamic-update-slice_fusion.4
  396.2 3.0 copy.125
  399.2 0.8 div.37
  400.0 1.6 fusion.60
  (86 shorter events, 7.8 us)
Async XLA Ops:
  7.2 7.1 %copy-start = (bf16[256,3072]{1,0:T(8,128)(2,1)S(1)}, bf16[256,3072]{1,0:T(8,128)(2,1)}, u32[]{:S(2)}) copy-start(bf16[256,3072]{1,0:T(8,128)(2,1)} %param.14) | copy-start | bytes 4718596
  7.2 392.0 %reduce-scatter.7.cloned.1.call-start = ((), (), s32[]{:S(2)}) async-start(), calls=%async_computation.3 | async-start | bytes 139264 | tf_op jit(solution)/shard_map/reduce_scatter | solution.py:131
  7.2 118.6 %collective-permute-start.6 = (s32[2]{0:T(128)}, s32[2]{0:T(128)S(1)}, u32[]{:S(2)}, u32[]{:S(2)}) collective-permute-start(s32[2]{0:T(128)} %param.18), channel_id=1, source_target_pairs={{0,1},{1,2},{2,3},{3,4},{4,5},{5,6},{6,7},{7,8},{8,9},{9,10},{10,1... | collective-permute-start | bytes 32 | tf_op jit(solution)/shard_map/ppermute | solution.py:16
  7.3 127.0 %collective-permute-start.7 = (s32[2]{0:T(128)}, s32[2]{0:T(128)S(1)}, u32[]{:S(2)}, u32[]{:S(2)}) collective-permute-start(s32[2]{0:T(128)} %param.18), channel_id=1, source_target_pairs={{0,15},{1,0},{2,1},{3,2},{4,3},{5,4},{6,5},{7,6},{8,7},{9,8},{10,9... | collective-permute-start | bytes 32 | tf_op jit(solution)/shard_map/ppermute | solution.py:16
  9.9 124.4 %collective-permute-start.4 = (s32[2]{0:T(128)}, s32[2]{0:T(128)S(1)}, u32[]{:S(2)}, u32[]{:S(2)}) collective-permute-start(s32[2]{0:T(128)} %param.18), channel_id=1, source_target_pairs={{0,4},{1,5},{2,6},{3,7},{4,8},{5,9},{6,10},{7,11},{8,12},{9,13},{1... | collective-permute-start | bytes 32 | tf_op jit(solution)/shard_map/ppermute | solution.py:16
  11.5 125.4 %collective-permute-start.5 = (s32[2]{0:T(128)}, s32[2]{0:T(128)S(1)}, u32[]{:S(2)}, u32[]{:S(2)}) collective-permute-start(s32[2]{0:T(128)} %param.18), channel_id=1, source_target_pairs={{0,12},{1,13},{2,14},{3,15},{4,0},{5,1},{6,2},{7,3},{8,4},{9,5},{1... | collective-permute-start | bytes 32 | tf_op jit(solution)/shard_map/ppermute | solution.py:16
  11.9 125.7 %collective-permute-start.8 = (bf16[2,128,3072]{2,1,0:T(8,128)(2,1)}, bf16[2,128,3072]{2,1,0:T(8,128)(2,1)}, u32[]{:S(2)}, u32[]{:S(2)}) collective-permute-start(bf16[2,128,3072]{2,1,0:T(8,128)(2,1)} %bitcast.13), channel_id=1, source_target_pairs={{0,4},{1,5},{2,6},{3,7},{4,8},{5,9},{6,10},{7,11},{8,12},{9,13},{1... | collective-permute-start | bytes 4718600 | tf_op jit(solution)/shard_map/ppermute | solution.py:16
  98.6 300.6 %reduce-scatter.5.cloned.1.call-start = ((), (), s32[]{:S(2)}) async-start(), calls=%async_computation.2 | async-start | bytes 3342336 | tf_op jit(solution)/shard_map/reduce_scatter | solution.py:130
  110.0 0.7 copy-start.10
  110.0 1.4 copy-start.7
  114.7 4.5 %copy-start.8 = (s32[2,6]{1,0:T(2,128)S(1)}, s32[2,6]{1,0:T(2,128)}, u32[]{:S(2)}) copy-start(s32[2,6]{1,0:T(2,128)} %param.17) | copy-start | bytes 148
  125.8 50.4 %collective-permute-start.9 = (bf16[2,128,3072]{2,1,0:T(8,128)(2,1)}, bf16[2,128,3072]{2,1,0:T(8,128)(2,1)}, u32[]{:S(2)}, u32[]{:S(2)}) collective-permute-start(bf16[2,128,3072]{2,1,0:T(8,128)(2,1)} %bitcast.13), channel_id=1, source_target_pairs={{0,12},{1,13},{2,14},{3,15},{4,0},{5,1},{6,2},{7,3},{8,4},{9,5},{1... | collective-permute-start | bytes 4718600 | tf_op jit(solution)/shard_map/ppermute | solution.py:16
  134.3 68.6 %collective-permute-start.10 = (bf16[2,128,3072]{2,1,0:T(8,128)(2,1)}, bf16[2,128,3072]{2,1,0:T(8,128)(2,1)}, u32[]{:S(2)}, u32[]{:S(2)}) collective-permute-start(bf16[2,128,3072]{2,1,0:T(8,128)(2,1)} %bitcast.13), channel_id=1, source_target_pairs={{0,1},{1,2},{2,3},{3,4},{4,5},{5,6},{6,7},{7,8},{8,9},{9,10},{10,1... | collective-permute-start | bytes 4718600 | tf_op jit(solution)/shard_map/ppermute | solution.py:16
  134.3 97.9 %collective-permute-start.11 = (bf16[2,128,3072]{2,1,0:T(8,128)(2,1)}, bf16[2,128,3072]{2,1,0:T(8,128)(2,1)}, u32[]{:S(2)}, u32[]{:S(2)}) collective-permute-start(bf16[2,128,3072]{2,1,0:T(8,128)(2,1)} %bitcast.13), channel_id=1, source_target_pairs={{0,15},{1,0},{2,1},{3,2},{4,3},{5,4},{6,5},{7,6},{8,7},{9,8},{10,9... | collective-permute-start | bytes 4718600 | tf_op jit(solution)/shard_map/ppermute | solution.py:16
  136.9 98.1 %collective-permute-start = (bf16[2,128,3072]{2,1,0:T(8,128)(2,1)}, bf16[2,128,3072]{2,1,0:T(8,128)(2,1)}, u32[]{:S(2)}, u32[]{:S(2)}) collective-permute-start(bf16[2,128,3072]{2,1,0:T(8,128)(2,1)} %bitcast.1), channel_id=1, source_target_pairs={{0,4},{1,5},{2,6},{3,7},{4,8},{5,9},{6,10},{7,11},{8,12},{9,13},{1... | collective-permute-start | bytes 4718600 | tf_op jit(solution)/shard_map/ppermute | solution.py:16
  137.7 117.5 %collective-permute-start.1 = (bf16[2,128,3072]{2,1,0:T(8,128)(2,1)}, bf16[2,128,3072]{2,1,0:T(8,128)(2,1)S(1)}, u32[]{:S(2)}, u32[]{:S(2)}) collective-permute-start(bf16[2,128,3072]{2,1,0:T(8,128)(2,1)} %bitcast.1), channel_id=1, source_target_pairs={{0,12},{1,13},{2,14},{3,15},{4,0},{5,1},{6,2},{7,3},{8,4},{9,5},{1... | collective-permute-start | bytes 4718600 | tf_op jit(solution)/shard_map/ppermute | solution.py:16
  176.2 105.2 %collective-permute-start.2 = (bf16[2,128,3072]{2,1,0:T(8,128)(2,1)}, bf16[2,128,3072]{2,1,0:T(8,128)(2,1)S(1)}, u32[]{:S(2)}, u32[]{:S(2)}) collective-permute-start(bf16[2,128,3072]{2,1,0:T(8,128)(2,1)} %bitcast.1), channel_id=1, source_target_pairs={{0,1},{1,2},{2,3},{3,4},{4,5},{5,6},{6,7},{7,8},{8,9},{9,10},{10,1... | collective-permute-start | bytes 4718600 | tf_op jit(solution)/shard_map/ppermute | solution.py:16
  176.2 58.8 %copy-start.6 = (bf16[5,2,128,3072]{3,2,1,0:T(8,128)(2,1)S(1)}, bf16[5,2,128,3072]{3,2,1,0:T(8,128)(2,1)}, u32[]{:S(2)}) copy-start(bf16[5,2,128,3072]{3,2,1,0:T(8,128)(2,1)} %constant_dynamic-update-slice_fusion.1) | copy-start | bytes 23592964
  202.8 78.7 %collective-permute-start.3 = (bf16[2,128,3072]{2,1,0:T(8,128)(2,1)}, bf16[2,128,3072]{2,1,0:T(8,128)(2,1)S(1)}, u32[]{:S(2)}, u32[]{:S(2)}) collective-permute-start(bf16[2,128,3072]{2,1,0:T(8,128)(2,1)} %bitcast.1), channel_id=1, source_target_pairs={{0,15},{1,0},{2,1},{3,2},{4,3},{5,4},{6,5},{7,6},{8,7},{9,8},{10,9... | collective-permute-start | bytes 4718600 | tf_op jit(solution)/shard_map/ppermute | solution.py:16
  297.2 4.4 %copy-start.5 = (bf16[2,128,24,128]{3,2,1,0:T(8,128)(2,1)S(1)}, bf16[2,128,24,128]{3,2,1,0:T(8,128)(2,1)}, u32[]{:S(2)}) copy-start(bf16[2,128,24,128]{3,2,1,0:T(8,128)(2,1)} %get-tuple-element.288) | copy-start | bytes 4718596 | tf_op jit(solution)/shard_map/while
  304.1 4.1 copy-start.2
  308.2 1.4 copy-start.3
  320.7 8.2 %copy-start.4 = (f32[24,128,128]{1,2,0:T(8,128)S(1)}, f32[24,128,128]{1,2,0:T(8,128)}, u32[]{:S(2)}) copy-start(f32[24,128,128]{1,2,0:T(8,128)} %fusion.96) | copy-start | bytes 4718596 | tf_op jit(solution)/shard_map/while
  351.5 4.3 %copy-start.5 = (bf16[2,128,24,128]{3,2,1,0:T(8,128)(2,1)S(1)}, bf16[2,128,24,128]{3,2,1,0:T(8,128)(2,1)}, u32[]{:S(2)}) copy-start(bf16[2,128,24,128]{3,2,1,0:T(8,128)(2,1)} %get-tuple-element.288) | copy-start | bytes 4718596 | tf_op jit(solution)/shard_map/while
  358.4 4.1 copy-start.2
  362.5 1.4 copy-start.3
  375.0 8.2 %copy-start.4 = (f32[24,128,128]{1,2,0:T(8,128)S(1)}, f32[24,128,128]{1,2,0:T(8,128)}, u32[]{:S(2)}) copy-start(f32[24,128,128]{1,2,0:T(8,128)} %fusion.96) | copy-start | bytes 4718596 | tf_op jit(solution)/shard_map/while
  396.2 3.8 copy-start.9
  396.2 5.5 %copy-start.1 = (bf16[256,3072]{1,0:T(8,128)(2,1)S(1)}, bf16[256,3072]{1,0:T(8,128)(2,1)}, u32[]{:S(2)}) copy-start(bf16[256,3072]{1,0:T(8,128)(2,1)} %param.14) | copy-start | bytes 4718596
Sparse Core Ops, SparseCore 0:
  98.7 115.0 reduce-scatter.6
  217.6 82.0 reduce-scatter.4
where the time goes:
time: 411 us; the launch traced here: 409 us
  waiting for transfers between devices  120 us (29%)
  local copies, waits for them, and re-layouts  119 us (29%)
  blocking collectives  74.3 us (18%)
  matrix products  43.2 us (11%)
  starting transfers between devices  19.5 us (5%)
  other arithmetic  17.8 us (4%)
  between operations  14.9 us (4%)
    ppermute x12, waiting for transfers between devices, passed_along(): lax.ppermute(x, axis, [(i, (i + by) % length) for i in range(length)])  120 us
    pmax x1, blocking collectives, per_device(): global_top = lax.pmax(local_top, 'tiles')  74.3 us
    unnamed x30, local copies, waits for them, and re-layouts  28.1 us
    while x20, local copies, waits for them, and re-layouts  22.8 us
    dot_general x2, matrix products, one_tile(): jnp.einsum('hqk,khd->qhd', video_probs.astype(jnp.bfloat16), values_chose...  21.1 us
    ppermute x12, starting transfers between devices, passed_along(): lax.ppermute(x, axis, [(i, (i + by) % length) for i in range(length)])  19.4 us
    gather x2, local copies, waits for them, and re-layouts, one_tile(): keys_chosen = key_flat[flat_row].reshape(-1, HEADS, HD)  17.7 us
    gather x2, local copies, waits for them, and re-layouts, one_tile(): values_chosen = value_flat[flat_row].reshape(-1, HEADS, HD)  17.5 us
  transfers between devices with their start and end apart: 14, of which 5 were waited for; matrix products, arithmetic and copies ran while one was open for 43% of the time, Pallas kernels for 0%

commit v1 on v0

v1 whole, which is shorter than its diff:
```python
import functools
import math

import jax
import jax.numpy as jnp
from jax import lax
from jax.experimental import pallas as pl
from jax.experimental.pallas import tpu as pltpu
from jax.sharding import PartitionSpec as P

HEADS = 24
HD = 128
NR = 4
WIDTH = 256
LOG2E_SCALE = math.log2(math.e) / math.sqrt(HD)
MESH = pl.DeviceIdType.MESH
NT = (((1,), (1,)), ((), ()))


def text_kernel(q_ref, k_ref, v_ref, bias_ref, num_ref, stat_ref):
    step = pl.program_id(0)

    @pl.when(step == 0)
    def _():
        stat_ref[...] = jnp.zeros_like(stat_ref)

    lanes = lax.broadcasted_iota(jnp.int32, stat_ref.shape, 1)
    bias = bias_ref[0:1, :]
    for h in range(WIDTH // HD):
        cols = slice(h * HD, (h + 1) * HD)
        s = lax.dot_general(
            q_ref[:, cols], k_ref[:, cols], NT, preferred_element_type=jnp.float32
        )
        s = s + bias
        top = jnp.max(s, axis=1, keepdims=True)
        p = jnp.exp2((s - top) * LOG2E_SCALE)
        total = jnp.sum(p, axis=1, keepdims=True)
        num = jnp.dot(p.astype(jnp.bfloat16), v_ref[:, cols], preferred_element_type=jnp.float32)
        num_ref[:, cols] = num.astype(jnp.bfloat16)
        head = step * (WIDTH // HD) + h
        stat = jnp.where(lanes == head, top, stat_ref[...])
        stat_ref[...] = jnp.where(lanes == head + 32, total, stat)


def main_kernel(
    n, q_ref, k_ref, v_ref, tk_ref, tv_ref, pick_ref, own_ref, qv_ref, tnum_ref, tstat_ref,
    out_ref, rnum_ref, rstat_ref,
    near, near_bias, send_sem, recv_sem, bsend_sem, brecv_sem, tsend_sem, trecv_sem, own_sem,
):
    group = lax.axis_index("groups")
    me = lax.axis_index("tiles")
    spot = lax.rem(me + n // 2 + NR + NR // 2, n)
    row = lax.rem(spot, NR)
    time = lax.div(spot, NR)
    chunks = q_ref.shape[1] // WIDTH
    has = (time > 0, time < n // NR - 1, row > 0, row < NR - 1)
    sends = (has[1], has[0], has[3], has[2])
    offs = (-NR, NR, -1, 1)
    targets = tuple((group, lax.rem(me - o + n, n)) for o in offs)

    barrier = pltpu.get_barrier_semaphore()

    def greet(i, _):
        pl.semaphore_signal(
            barrier, inc=1, device_id=(group, lax.rem(me + i, n)), device_id_type=MESH
        )
        return 0

    lax.fori_loop(1, n, greet, 0)
    pl.semaphore_wait(barrier, n - 1)

    def bias_copy(d):
        return pltpu.make_async_remote_copy(
            src_ref=own_ref, dst_ref=near_bias.at[d], send_sem=bsend_sem.at[d],
            recv_sem=brecv_sem.at[d], device_id=targets[d], device_id_type=MESH,
        )

    def block_copy(d, kv, c):
        cols = pl.ds(pl.multiple_of(c * WIDTH, WIDTH), WIDTH)
        return pltpu.make_async_remote_copy(
            src_ref=(k_ref, v_ref)[kv].at[:, cols], dst_ref=near.at[d, kv, c],
            send_sem=send_sem.at[d, kv, c], recv_sem=recv_sem.at[d, kv, c],
            device_id=targets[d], device_id_type=MESH,
        )

    def text_copies(i):
        to = lax.rem(me + i, n)
        return (
            pltpu.make_async_remote_copy(
                src_ref=tnum_ref.at[to], dst_ref=rnum_ref.at[me], send_sem=tsend_sem.at[0, i],
                recv_sem=trecv_sem.at[0, i], device_id=(group, to), device_id_type=MESH,
            ),
            pltpu.make_async_remote_copy(
                src_ref=tstat_ref.at[to], dst_ref=rstat_ref.at[me], send_sem=tsend_sem.at[1, i],
                recv_sem=trecv_sem.at[1, i], device_id=(group, to), device_id_type=MESH,
            ),
        )

    def text_arrivals(i):
        origin = lax.rem(me - i + n, n)
        return (
            pltpu.make_async_remote_copy(
                src_ref=tnum_ref.at[origin], dst_ref=rnum_ref.at[origin],
                send_sem=tsend_sem.at[0, i], recv_sem=trecv_sem.at[0, i],
                device_id=(group, origin), device_id_type=MESH,
            ),
            pltpu.make_async_remote_copy(
                src_ref=tstat_ref.at[origin], dst_ref=rstat_ref.at[origin],
                send_sem=tsend_sem.at[1, i], recv_sem=trecv_sem.at[1, i],
                device_id=(group, origin), device_id_type=MESH,
            ),
        )

    for d in range(4):
        @pl.when(sends[d])
        def _(d=d):
            bias_copy(d).start()

    def start_chunk(c, _):
        for d in range(4):
            @pl.when(sends[d])
            def _(d=d):
                block_copy(d, 0, c).start()
                block_copy(d, 1, c).start()
        return 0

    lax.fori_loop(0, chunks, start_chunk, 0)

    def start_text(i, _):
        for copy in text_copies(i):
            copy.start()
        return 0

    lax.fori_loop(1, n, start_text, 0)
    own_num = pltpu.make_async_copy(tnum_ref.at[me], rnum_ref.at[me], own_sem.at[0])
    own_stat = pltpu.make_async_copy(tstat_ref.at[me], rstat_ref.at[me], own_sem.at[1])
    own_num.start()
    own_stat.start()

    for d in range(4):
        @pl.when(jnp.logical_not(has[d]))
        def _(d=d):
            near_bias[d] = jnp.full(near_bias.shape[1:], -jnp.inf, jnp.float32)

            def clear(c, _):
                near[d, 0, c] = jnp.zeros(near.shape[3:], jnp.bfloat16)
                near[d, 1, c] = jnp.zeros(near.shape[3:], jnp.bfloat16)
                return 0

            lax.fori_loop(0, chunks, clear, 0)

        @pl.when(has[d])
        def _(d=d):
            bias_copy(d).wait_recv()

    tokens = q_ref.shape[0]
    half = tokens // 2

    def attend(c, _):
        for d in range(4):
            @pl.when(has[d])
            def _(d=d):
                block_copy(d, 0, c).wait_recv()
                block_copy(d, 1, c).wait_recv()
        for h in range(WIDTH // HD):
            cols = pl.ds(pl.multiple_of(c * WIDTH + h * HD, HD), HD)
            here = slice(h * HD, (h + 1) * HD)
            q = q_ref[:, cols]
            scores = []
            for b in range(6):
                if b == 0:
                    key, extra = k_ref[:, cols], own_ref[0:1, :]
                elif b == 5:
                    key, extra = tk_ref[:, cols], None
                else:
                    key, extra = near[b - 1, 0, c, :, here], near_bias[b - 1, 0:1, :]
                s = lax.dot_general(q, key, NT, preferred_element_type=jnp.float32)
                parts = []
                for t in range(2):
                    bias = pick_ref[b, t:t + 1, :]
                    if extra is not None:
                        bias = bias + extra
                    parts.append(s[t * half:(t + 1) * half] + bias)
                scores.append(jnp.concatenate(parts, axis=0))
            top = functools.reduce(jnp.maximum, scores)
            top = jnp.max(top, axis=1, keepdims=True)
            total, num = None, None
            for b in range(6):
                p = jnp.exp2((scores[b] - top) * LOG2E_SCALE)
                total = p if total is None else total + p
                if b == 0:
                    value = v_ref[:, cols]
                elif b == 5:
                    value = tv_ref[:, cols]
                else:
                    value = near[b - 1, 1, c, :, here]
                term = jnp.dot(p.astype(jnp.bfloat16), value, preferred_element_type=jnp.float32)
                num = term if num is None else num + term
            total = jnp.sum(total, axis=1, keepdims=True)
            result = jnp.where(qv_ref[...] > 0, num / total, 0.0)
            out_ref[:, cols] = result.astype(jnp.bfloat16)
        return 0

    lax.fori_loop(0, chunks, attend, 0)

    for d in range(4):
        @pl.when(sends[d])
        def _(d=d):
            bias_copy(d).wait_send()

    def finish_chunk(c, _):
        for d in range(4):
            @pl.when(sends[d])
            def _(d=d):
                block_copy(d, 0, c).wait_send()
                block_copy(d, 1, c).wait_send()
        return 0

    lax.fori_loop(0, chunks, finish_chunk, 0)

    def finish_text(i, _):
        for copy in text_arrivals(i):
            copy.wait_recv()
        for copy in text_copies(i):
            copy.wait_send()
        return 0

    lax.fori_loop(1, n, finish_text, 0)
    own_num.wait()
    own_stat.wait()


def per_device(video_q, video_k, video_v, text_q, text_k, text_v, window, counts, text_count):
    n = lax.axis_size("tiles")
    position = lax.axis_index("tiles")
    tiles = counts.shape[0]
    tokens, width = video_q.shape
    tok = tokens // tiles
    text = text_q.shape[0]
    share = text // n
    slots = jnp.arange(tok, dtype=jnp.int32)
    valid = (slots[None, :] < counts[:, None]).reshape(-1)
    own_bias = jnp.broadcast_to(jnp.where(valid, 0.0, -jnp.inf)[None, :], (8, tokens))
    codes = jnp.concatenate([jnp.ones((tiles, 1), jnp.int32), window + (window >= 1)], axis=1)
    column = jnp.arange(tiles, dtype=jnp.int32)[:, None] + codes % 3 - 1
    block_ids = jnp.arange(5, dtype=jnp.int32)[:, None, None, None]
    column_ids = jnp.arange(tiles, dtype=jnp.int32)[None, None, :, None]
    hit = jnp.any(
        (codes[None, :, None, :] // 3 == block_ids) & (column[None, :, None, :] == column_ids),
        axis=-1,
    )
    pick = jnp.broadcast_to(hit[..., None], (5, tiles, tiles, tok)).reshape(5, tiles, tokens)
    text_ok = jnp.arange(text, dtype=jnp.int32) < text_count[0]
    text_pick = jnp.broadcast_to(text_ok[None, None, :], (1, tiles, text))
    pick = jnp.where(jnp.concatenate([pick, text_pick], axis=0), 0.0, -jnp.inf)
    pick = jnp.pad(pick, ((0, 0), (0, 8 - tiles), (0, 0)))
    query_valid = valid.astype(jnp.float32)[:, None]

    step_in = pl.BlockSpec((tokens, WIDTH), lambda i: (0, i))
    text_step = pl.BlockSpec((text, WIDTH), lambda i: (0, i))
    tnum, tstat = pl.pallas_call(
        text_kernel,
        grid=(width // WIDTH,),
        out_shape=(
            jax.ShapeDtypeStruct((text, width), jnp.bfloat16),
            jax.ShapeDtypeStruct((text, 128), jnp.float32),
        ),
        in_specs=[text_step, step_in, step_in, pl.BlockSpec((8, tokens), lambda i: (0, 0))],
        out_specs=(text_step, pl.BlockSpec((text, 128), lambda i: (0, 0))),
    )(text_q, video_k, video_v, own_bias)

    vmem = pl.BlockSpec(memory_space=pltpu.VMEM)
    hbm = pl.BlockSpec(memory_space=pl.ANY)
    chunks = width // WIDTH
    dma = pltpu.SemaphoreType.DMA
    video_out, rnum, rstat = pl.pallas_call(
        functools.partial(main_kernel, n),
        out_shape=(
            jax.ShapeDtypeStruct((tokens, width), jnp.bfloat16),
            jax.ShapeDtypeStruct((n, share, width), jnp.bfloat16),
            jax.ShapeDtypeStruct((n, share, 128), jnp.float32),
        ),
        in_specs=[vmem] * 8 + [hbm, hbm],
        out_specs=(vmem, hbm, hbm),
        scratch_shapes=[
            pltpu.VMEM((4, 2, chunks, tokens, WIDTH), jnp.bfloat16),
            pltpu.VMEM((4, 8, tokens), jnp.float32),
            dma((4, 2, chunks)),
            dma((4, 2, chunks)),
            dma((4,)),
            dma((4,)),
            dma((2, n)),
            dma((2, n)),
            dma((2,)),
        ],
        compiler_params=pltpu.CompilerParams(
            collective_id=0, has_side_effects=True, vmem_limit_bytes=48 * 1024 * 1024
        ),
    )(
        video_q, video_k, video_v, text_k, text_v, pick, own_bias, query_valid,
        tnum.reshape(n, share, width), tstat.reshape(n, share, 128),
    )

    tops, sums = rstat[..., :HEADS], rstat[..., 32:32 + HEADS]
    scale = jnp.exp2((tops - jnp.max(tops, axis=0)) * LOG2E_SCALE)
    den = jnp.sum(sums * scale, axis=0)
    parts = rnum.reshape(n, share, HEADS, HD).astype(jnp.float32)
    text_result = jnp.sum(parts * scale[..., None], axis=0) / den[..., None]
    row_ids = position * share + jnp.arange(share, dtype=jnp.int32)
    text_out = jnp.where((row_ids < text_count[0])[:, None, None], text_result, 0.0)
    return (video_out, text_out.astype(jnp.bfloat16).reshape(share, width))


def solution(mesh):
    return jax.shard_map(
        per_device,
        mesh=mesh,
        in_specs=(
            P(("groups", "tiles"), None),
            P(("groups", "tiles"), None),
            P(("groups", "tiles"), None),
            P("groups", None),
            P("groups", None),
            P("groups", None),
            P("tiles", None),
            P(("groups", "tiles")),
            P("groups"),
        ),
        out_specs=(P(("groups", "tiles"), None), P(("groups", "tiles"), None)),
        check_vma=False,
    )
```

time: 411 us -> 247 us (0.60)
  Pallas kernels: 0 us -> 228 us
  waiting for transfers between devices: 120 us -> 0 us
  local copies, waits for them, and re-layouts: 119 us -> 11.3 us
  blocking collectives: 74.3 us -> 0 us
  matrix products: 43.2 us -> 0 us
  starting transfers between devices: 19.5 us -> 0 us
  between operations: 14.9 us -> 1.4 us
  other arithmetic: 17.8 us -> 4.88 us
    pallas_call x0 -> x2, Pallas kernels: none -> 228 us  [the longest x1 216 us: per_device(): pl.pallas_call(functools.partial(main_kernel, n), out_shape=(jax.ShapeDty...]
    ppermute x12 -> x0, waiting for transfers between devices: 120 us -> none  [passed_along(): lax.ppermute(x, axis, [(i, (i + by) % length) for i in range(length)])]
    pmax x1 -> x0, blocking collectives: 74.3 us -> none  [per_device(): global_top = lax.pmax(local_top, 'tiles')]
    dot_general x10 -> x0, matrix products: 43.2 us -> none  [the longest x2 21.1 us: one_tile(): jnp.einsum('hqk,khd->qhd', video_probs.astype(jnp.bfloat16), values_chose...]
    gather x6 -> x0, local copies, waits for them, and re-layouts: 36.5 us -> none  [the longest x2 17.7 us: one_tile(): keys_chosen = key_flat[flat_row].reshape(-1, HEADS, HD)]
    unnamed x30 -> x9, local copies, waits for them, and re-layouts: 28.1 us -> 3.46 us
    while x20 -> x0, local copies, waits for them, and re-layouts: 22.8 us -> none
    ppermute x12 -> x0, starting transfers between devices: 19.4 us -> none  [passed_along(): lax.ppermute(x, axis, [(i, (i + by) % length) for i in range(length)])]
  transfers between devices with their start and end apart: 14 -> 0, of which waited for: 5 -> 0; matrix products, arithmetic and copies ran while one was open for 43% -> 0% of each run, Pallas kernels for 0% -> 0%
where the time goes in v1:
time: 247 us; the launch traced here: 246 us
  Pallas kernels  228 us (92%)
  local copies, waits for them, and re-layouts  11.3 us (5%)
  other arithmetic  4.88 us (2%)
    pallas_call x1, Pallas kernels, per_device(): pl.pallas_call(functools.partial(main_kernel, n), out_shape=(jax.ShapeDty...  216 us
    pallas_call x1, Pallas kernels, per_device(): pl.pallas_call(text_kernel, grid=(width // WIDTH,), out_shape=(jax.ShapeD...  12.2 us
    mul x2, local copies, waits for them, and re-layouts, per_device(): text_result = jnp.sum(parts * scale[..., None], axis=0) / den[..., None]  6.7 us

profile of v1, /device:TPU:8, one launch (start us, length us, event | category | flops | bytes accessed | tf_op | source)
XLA Modules:
  0.0 245.8 jit_solution(18033167020236047732)
XLA Ops:
  0.6 0.7 fusion.2
  1.3 0.1 and_select_fusion.1
  1.4 0.1 and_reduce_fusion
  1.6 0.1 copy.13
  1.7 0.1 broadcast_in_dim.30
  2.5 0.7 select_bitcast_fusion
  3.3 0.6 broadcast_in_dim.64.bias_ref.own_ref
  3.9 0.0 copy-start.3
  3.9 0.0 copy-start.2
  3.9 12.2 %shard_map.104 = (bf16[256,3072]{1,0:T(8,128)(2,1)}, f32[256,128]{1,0:T(8,128)}) custom-call(bf16[256,3072]{1,0:T(8,128)(2,1)} %q_ref.2, bf16[256,3072]{1,0:T(8,128)(2,1)} %k_ref.3, bf16[256,3072]{1,0:T(8,128)(2,1)} %v_ref.3, f32[8,256]{1,0:T(8,128)} %broadcast_in_dim.64.bias_ref.own_ref), custom_call_target="tpu_custom_call" | custom-call | tf_op jit(solution)/shard_map/pallas_call | solution.py:261
  16.1 0.0 copy-done.3
  16.1 0.1 fusion.4
  16.1 0.1 copy.15.qv_ref
  16.3 0.0 copy-done.2
  16.3 0.0 copy-start
  16.3 1.4 copy-done
  17.7 0.0 copy-start.1
  17.7 0.9 copy-done.1
  18.6 216.0 %shard_map.105 = (bf16[256,3072]{1,0:T(8,128)(2,1)S(1)}, bf16[16,16,3072]{2,1,0:T(8,128)(2,1)S(1)}, f32[16,16,128]{2,1,0:T(8,128)S(1)}) custom-call(bf16[256,3072]{1,0:T(8,128)(2,1)S(1)} %copy-done, bf16[256,3072]{1,0:T(8,128)(2,1)} %k_ref.3, bf16[256,3072]{1,0:T(8,128)(2,1)} %v_ref.3, bf16[256,3072]{1,0:T(8,128)(2,1)} %tk_ref.1, bf16[256,3072]{1,0:T(8,128)(2,1)} %tv_ref.1, ...), custom_call_target="tpu_custom_call" | custom-call | tf_op jit(solution)/shard_map/pallas_call | solution.py:276
  234.7 0.1 multiply_reduce_fusion.1
  234.8 2.2 mul.20
  236.9 4.5 %mul.21 = f32[16,16,3072]{2,1,0:T(8,128)} reshape(f32[16,16,24,128]{3,2,1,0:T(8,128)} %mul.20) | data formatting | bytes 6291456 | tf_op jit(solution)/shard_map/mul | solution.py:308
  241.5 2.3 multiply_reduce_fusion
  243.8 0.1 div.19
  243.9 0.7 fusion.1
  244.6 1.1 copy.20
  (10 shorter events, 0.1 us)
Async XLA Ops:
  3.9 12.2 %copy-start.3 = (s32[2]{0:T(128)S(1)}, s32[2]{0:T(128)}, u32[]{:S(2)}) copy-start(s32[2]{0:T(128)} %param.16) | copy-start | bytes 28
  3.9 12.4 %copy-start.2 = (f32[8,256]{1,0:T(8,128)S(1)}, f32[8,256]{1,0:T(8,128)}, u32[]{:S(2)}) copy-start(f32[8,256]{1,0:T(8,128)} %broadcast_in_dim.64.bias_ref.own_ref) | copy-start | bytes 24580
  16.3 1.4 copy-start
  17.7 0.9 copy-start.1

commit v2 on v1

v2 whole, which is shorter than its diff:
```python
import functools
import math

import jax
import jax.numpy as jnp
from jax import lax
from jax.experimental import pallas as pl
from jax.experimental.pallas import tpu as pltpu
from jax.sharding import PartitionSpec as P

HEADS = 24
HD = 128
NR = 4
WIDTH = 256
LOG2E_SCALE = math.log2(math.e) / math.sqrt(HD)
MESH = pl.DeviceIdType.MESH
NT = (((1,), (1,)), ((), ()))


def main_kernel(
    n, q_ref, k_ref, v_ref, tq_ref, tk_ref, tv_ref, pick_ref, own_ref, qv_ref, tok_ref,
    out_ref, tout_ref,
    near, near_bias, relay, tnum, tstat, rnum, rstat,
    send_sem, recv_sem, bsend_sem, brecv_sem, fsend_sem, rsend_sem, rrecv_sem, tsend_sem, trecv_sem,
):
    group = lax.axis_index("groups")
    me = lax.axis_index("tiles")
    last = n // NR - 1
    chunks = q_ref.shape[1] // WIDTH
    per_chunk = WIDTH // HD
    tokens = q_ref.shape[0]
    half = tokens // 2
    share = tout_ref.shape[0]

    def at(offset):
        return lax.rem(me + offset + n, n)

    def time_of(index):
        return lax.div(lax.rem(index + n // 2 + NR + NR // 2, n), NR)

    row = lax.rem(me + n // 2 + NR + NR // 2, NR)
    time = time_of(me)
    side = lax.rem(me, 2)
    has = (time > 0, time < last, row > 0, row < NR - 1)
    offs = (-NR, NR, -1, 1)
    even = lax.rem(row, 2) == 0
    odd = lax.rem(row, 2) == 1
    quarter = lax.rem(me, 4)
    wrap_up = (quarter == 1) & (me < NR) & (time > 0)
    wrap_down = (quarter == 1) & (me >= n - NR) & (time < last)
    relay_up = (quarter == 3) & (me < NR) & (time_of(at(-2)) > 0)
    relay_down = (quarter == 3) & (me >= n - NR) & (time_of(at(-2)) < last)
    forward_down = (row == 1) & (time > 0)
    forward_up = (row == 2) & (time < last)

    barrier = pltpu.get_barrier_semaphore()

    def greet(i, _):
        pl.semaphore_signal(barrier, inc=1, device_id=(group, at(i)), device_id_type=MESH)
        return 0

    lax.fori_loop(1, n, greet, 0)
    pl.semaphore_wait(barrier, n - 1)

    def remote(source, target, sent, got, to):
        return pltpu.make_async_remote_copy(
            src_ref=source, dst_ref=target, send_sem=sent, recv_sem=got,
            device_id=(group, to), device_id_type=MESH,
        )

    def block(kv, c):
        cols = pl.ds(pl.multiple_of(c * WIDTH, WIDTH), WIDTH)
        return (k_ref, v_ref)[kv].at[:, cols]

    def bias_copy(d):
        return remote(own_ref, near_bias.at[d], bsend_sem.at[d], brecv_sem.at[d], at(-offs[d]))

    def direct(d, kv, c):
        return remote(
            block(kv, c), near.at[d, kv, c], send_sem.at[d, kv, c], recv_sem.at[d, kv, c], at(-offs[d])
        )

    def to_relay(d, kv, c):
        return remote(
            block(kv, c), relay.at[kv, c], send_sem.at[d, kv, c], rrecv_sem.at[kv, c], at(2)
        )

    def from_relay(d, kv, c):
        return remote(
            relay.at[kv, c], near.at[d, kv, c], rsend_sem.at[kv, c], recv_sem.at[d, kv, c],
            at(-2 - offs[d]),
        )

    def forward(d, kv, c):
        slot, to = (2, at(1 - NR)) if d == 0 else (3, at(NR - 1))
        return remote(
            near.at[d, kv, c], near.at[slot, kv, c], fsend_sem.at[kv, c], recv_sem.at[slot, kv, c], to
        )

    pair_sends = (((2, even), (0, 1)), ((3, odd), (0, 1)))
    far_sends = (
        ((0, (time < last) & jnp.logical_not(wrap_down)), (0, 1)),
        ((0, wrap_down), (1,)),
        ((1, (time > 0) & jnp.logical_not(wrap_up)), (0, 1)),
        ((2, (row == 1) & (time == last)), (0, 1)),
        ((3, (row == 2) & (time == 0)), (0, 1)),
    )
    relay_sends = (((0, wrap_down), (0,)), ((1, wrap_up), (0, 1)))
    onward = (((0, relay_down), (0,)), ((1, relay_up), (0, 1)))
    forwards = (((0, forward_down), (0, 1)), ((1, forward_up), (0, 1)))

    def each(table, make, act, c):
        for (d, when), kinds in table:
            @pl.when(when)
            def _(d=d, kinds=kinds):
                for kv in kinds:
                    act(make(d, kv, c))

    def start(copy):
        copy.start()

    def wait_send(copy):
        copy.wait_send()

    bias_sends = (has[1], has[0], has[3], has[2])
    for d in range(4):
        @pl.when(bias_sends[d])
        def _(d=d):
            bias_copy(d).start()

    def start_far(c, _):
        each(relay_sends, to_relay, start, c)
        each(far_sends, direct, start, c)

        def pass_on(d, kinds):
            for kv in kinds:
                pltpu.make_async_remote_copy(
                    src_ref=block(kv, c), dst_ref=relay.at[kv, c], send_sem=send_sem.at[d, kv, c],
                    recv_sem=rrecv_sem.at[kv, c], device_id=(group, at(2)), device_id_type=MESH,
                ).wait_recv()
                from_relay(d, kv, c).start()

        for (d, when), kinds in onward:
            @pl.when(when)
            def _(d=d, kinds=kinds):
                pass_on(d, kinds)
        return 0

    def start_pair(c, _):
        each(pair_sends, direct, start, c)
        return 0

    def missing(d):
        near_bias[d] = jnp.full(near_bias.shape[1:], -jnp.inf, jnp.float32)

        def clear(c, _):
            near[d, 0, c] = jnp.zeros(near.shape[3:], jnp.bfloat16)
            near[d, 1, c] = jnp.zeros(near.shape[3:], jnp.bfloat16)
            return 0

        lax.fori_loop(0, chunks, clear, 0)

    lax.fori_loop(0, 2, start_far, 0)
    lax.fori_loop(0, chunks, start_pair, 0)
    for d in range(4):
        @pl.when(jnp.logical_not(has[d]))
        def _(d=d):
            missing(d)

        @pl.when(has[d])
        def _(d=d):
            bias_copy(d).wait_recv()

    text_chunks = chunks // 2
    first = side * text_chunks
    lanes = lax.broadcasted_iota(jnp.int32, (share, 128), 1)

    def pair_arrived(c, _):
        for d, when in ((3, even), (2, odd)):
            @pl.when(when)
            def _(d=d):
                direct(d, 0, c).wait_recv()
                direct(d, 1, c).wait_recv()
        return 0

    lax.fori_loop(0, chunks, pair_arrived, 0)
    pair_slot = 3 - lax.rem(row, 2)
    tstat[...] = jnp.zeros_like(tstat)

    def text_part(j, _):
        c = first + j
        for h in range(per_chunk):
            cols = pl.ds(pl.multiple_of(c * WIDTH + h * HD, HD), HD)
            here = slice(h * HD, (h + 1) * HD)
            to = pl.ds(pl.multiple_of(j * WIDTH + h * HD, HD), HD)
            q = tq_ref[:, cols]
            s0 = lax.dot_general(q, k_ref[:, cols], NT, preferred_element_type=jnp.float32)
            s1 = lax.dot_general(
                q, near[pair_slot, 0, c, :, here], NT, preferred_element_type=jnp.float32
            )
            s0 = s0 + own_ref[0:1, :]
            s1 = s1 + near_bias[pair_slot, 0:1, :]
            top = jnp.max(jnp.maximum(s0, s1), axis=1, keepdims=True)
            p0 = jnp.exp2((s0 - top) * LOG2E_SCALE)
            p1 = jnp.exp2((s1 - top) * LOG2E_SCALE)
            total = jnp.sum(p0 + p1, axis=1, keepdims=True)
            num = None
            for p, value in ((p0, v_ref[:, cols]), (p1, near[pair_slot, 1, c, :, here])):
                high = p.astype(jnp.bfloat16)
                low = (p - high.astype(jnp.float32)).astype(jnp.bfloat16)
                for part in (high, low):
                    term = jnp.dot(part, value, preferred_element_type=jnp.float32)
                    num = term if num is None else num + term
            num = num.astype(jnp.bfloat16)
            head = j * per_chunk + h
            for b in range(n):
                rows = slice(b * share, (b + 1) * share)
                tnum[b, :, to] = num[rows]
                tstat[b, 0] = jnp.where(lanes == head, top[rows], tstat[b, 0])
                tstat[b, 1] = jnp.where(lanes == head, total[rows], tstat[b, 1])
        return 0

    lax.fori_loop(0, text_chunks, text_part, 0)

    def text_copies(i, there, here):
        return (
            remote(tnum.at[there], rnum.at[here], tsend_sem.at[0, i], trecv_sem.at[0, i], there),
            remote(tstat.at[there], rstat.at[here], tsend_sem.at[1, i], trecv_sem.at[1, i], there),
        )

    def start_text(i, _):
        for copy in text_copies(i, at(i), me):
            copy.start()
        return 0

    lax.fori_loop(1, n, start_text, 0)
    rnum[me] = tnum[me]
    rstat[me] = tstat[me]
    lax.fori_loop(2, chunks, start_far, 0)

    waits = (
        (0, has[0]), (1, has[1]),
        (2, has[2] & even), (3, has[3] & odd),
    )

    def attend(c, _):
        for d, when in waits[:2]:
            @pl.when(when)
            def _(d=d):
                direct(d, 0, c).wait_recv()
                direct(d, 1, c).wait_recv()
        each(forwards, forward, start, c)
        for d, when in waits[2:]:
            @pl.when(when)
            def _(d=d):
                direct(d, 0, c).wait_recv()
                direct(d, 1, c).wait_recv()
        for h in range(WIDTH // HD):
            cols = pl.ds(pl.multiple_of(c * WIDTH + h * HD, HD), HD)
            here = slice(h * HD, (h + 1) * HD)
            q = q_ref[:, cols]
            scores = []
            for b in range(6):
                if b == 0:
                    key, extra = k_ref[:, cols], own_ref[0:1, :]
                elif b == 5:
                    key, extra = tk_ref[:, cols], None
                else:
                    key, extra = near[b - 1, 0, c, :, here], near_bias[b - 1, 0:1, :]
                s = lax.dot_general(q, key, NT, preferred_element_type=jnp.float32)
                parts = []
                for t in range(2):
                    bias = pick_ref[b, t:t + 1, :]
                    if extra is not None:
                        bias = bias + extra
                    parts.append(s[t * half:(t + 1) * half] + bias)
                scores.append(jnp.concatenate(parts, axis=0))
            top = functools.reduce(jnp.maximum, scores)
            top = jnp.max(top, axis=1, keepdims=True)
            total, num = None, None
            for b in range(6):
                p = jnp.exp2((scores[b] - top) * LOG2E_SCALE)
                total = p if total is None else total + p
                if b == 0:
                    value = v_ref[:, cols]
                elif b == 5:
                    value = tv_ref[:, cols]
                else:
                    value = near[b - 1, 1, c, :, here]
                term = jnp.dot(p.astype(jnp.bfloat16), value, preferred_element_type=jnp.float32)
                num = term if num is None else num + term
            total = jnp.sum(total, axis=1, keepdims=True)
            result = jnp.where(qv_ref[...] > 0, num / total, 0.0)
            out_ref[:, cols] = result.astype(jnp.bfloat16)
        return 0

    lax.fori_loop(0, chunks, attend, 0)

    def finish(c, _):
        each(pair_sends, direct, wait_send, c)
        each(far_sends, direct, wait_send, c)
        each(relay_sends, to_relay, wait_send, c)
        each(onward, from_relay, wait_send, c)
        each(forwards, forward, wait_send, c)
        return 0

    def text_arrived(i, _):
        for copy in text_copies(i, at(n - i), at(n - i)):
            copy.wait_recv()
        for copy in text_copies(i, at(i), me):
            copy.wait_send()
        return 0

    lax.fori_loop(1, n, text_arrived, 0)

    heads = tnum.shape[2] // HD
    for e in range(2):
        top = lax.fori_loop(
            1, n // 2, lambda i, m: jnp.maximum(m, rstat[2 * i + e, 0]), rstat[e, 0]
        )

        def add(i, carry):
            den, nums = carry
            scale = jnp.exp2((rstat[2 * i + e, 0] - top) * LOG2E_SCALE)
            den = den + scale * rstat[2 * i + e, 1]
            nums = tuple(
                nums[j]
                + rnum[2 * i + e, :, j * HD:(j + 1) * HD].astype(jnp.float32) * scale[:, j:j + 1]
                for j in range(heads)
            )
            return den, nums

        zeros = jnp.zeros((share, HD), jnp.float32)
        den, nums = lax.fori_loop(0, n // 2, add, (zeros, (zeros,) * heads))
        for j in range(heads):
            result = jnp.where(tok_ref[...] > 0, nums[j] / den[:, j:j + 1], 0.0)
            at_head = (e * heads + j) * HD
            tout_ref[:, at_head:at_head + HD] = result.astype(jnp.bfloat16)

    for d in range(4):
        @pl.when(bias_sends[d])
        def _(d=d):
            bias_copy(d).wait_send()
    lax.fori_loop(0, chunks, finish, 0)


def per_device(video_q, video_k, video_v, text_q, text_k, text_v, window, counts, text_count):
    n = lax.axis_size("tiles")
    position = lax.axis_index("tiles")
    tiles = counts.shape[0]
    tokens, width = video_q.shape
    tok = tokens // tiles
    text = text_q.shape[0]
    share = text // n
    slots = jnp.arange(tok, dtype=jnp.int32)
    valid = (slots[None, :] < counts[:, None]).reshape(-1)
    own_bias = jnp.broadcast_to(jnp.where(valid, 0.0, -jnp.inf)[None, :], (8, tokens))
    codes = jnp.concatenate([jnp.ones((tiles, 1), jnp.int32), window + (window >= 1)], axis=1)
    column = jnp.arange(tiles, dtype=jnp.int32)[:, None] + codes % 3 - 1
    block_ids = jnp.arange(5, dtype=jnp.int32)[:, None, None, None]
    column_ids = jnp.arange(tiles, dtype=jnp.int32)[None, None, :, None]
    hit = jnp.any(
        (codes[None, :, None, :] // 3 == block_ids) & (column[None, :, None, :] == column_ids),
        axis=-1,
    )
    pick = jnp.broadcast_to(hit[..., None], (5, tiles, tiles, tok)).reshape(5, tiles, tokens)
    text_ok = jnp.arange(text, dtype=jnp.int32) < text_count[0]
    text_pick = jnp.broadcast_to(text_ok[None, None, :], (1, tiles, text))
    pick = jnp.where(jnp.concatenate([pick, text_pick], axis=0), 0.0, -jnp.inf)
    pick = jnp.pad(pick, ((0, 0), (0, 8 - tiles), (0, 0)))
    query_valid = valid.astype(jnp.float32)[:, None]

    row_ids = position * share + jnp.arange(share, dtype=jnp.int32)
    row_valid = (row_ids < text_count[0]).astype(jnp.float32)[:, None]
    vmem = pl.BlockSpec(memory_space=pltpu.VMEM)
    chunks = width // WIDTH
    dma = pltpu.SemaphoreType.DMA
    video_out, text_out = pl.pallas_call(
        functools.partial(main_kernel, n),
        out_shape=(
            jax.ShapeDtypeStruct((tokens, width), jnp.bfloat16),
            jax.ShapeDtypeStruct((share, width), jnp.bfloat16),
        ),
        in_specs=[vmem] * 10,
        out_specs=(vmem, vmem),
        scratch_shapes=[
            pltpu.VMEM((4, 2, chunks, tokens, WIDTH), jnp.bfloat16),
            pltpu.VMEM((4, 8, tokens), jnp.float32),
            pltpu.VMEM((2, chunks, tokens, WIDTH), jnp.bfloat16),
            pltpu.VMEM((n, share, width // 2), jnp.bfloat16),
            pltpu.VMEM((n, 2, share, 128), jnp.float32),
            pltpu.VMEM((n, share, width // 2), jnp.bfloat16),
            pltpu.VMEM((n, 2, share, 128), jnp.float32),
            dma((4, 2, chunks)),
            dma((4, 2, chunks)),
            dma((4,)),
            dma((4,)),
            dma((2, chunks)),
            dma((2, chunks)),
            dma((2, chunks)),
            dma((2, n)),
            dma((2, n)),
        ],
        compiler_params=pltpu.CompilerParams(
            collective_id=0, has_side_effects=True, vmem_limit_bytes=56 * 1024 * 1024
        ),
    )(
        video_q, video_k, video_v, text_q, text_k, text_v, pick, own_bias, query_valid, row_valid
    )
    return (video_out, text_out)


def solution(mesh):
    return jax.shard_map(
        per_device,
        mesh=mesh,
        in_specs=(
            P(("groups", "tiles"), None),
            P(("groups", "tiles"), None),
            P(("groups", "tiles"), None),
            P("groups", None),
            P("groups", None),
            P("groups", None),
            P("tiles", None),
            P(("groups", "tiles")),
            P("groups"),
        ),
        out_specs=(P(("groups", "tiles"), None), P(("groups", "tiles"), None)),
        check_vma=False,
    )
```

time: 247 us -> 175 us (0.71)
  Pallas kernels: 228 us -> 164 us
  local copies, waits for them, and re-layouts: 11.3 us -> 5.59 us
    pallas_call x1, Pallas kernels: 216 us -> 164 us  [per_device(): pl.pallas_call(functools.partial(main_kernel, n), out_shape=(jax.ShapeDty...]
    pallas_call x1 -> x0, Pallas kernels: 12.2 us -> none  [per_device(): pl.pallas_call(text_kernel, grid=(width // WIDTH,), out_shape=(jax.ShapeD...]
    mul x2 -> x0, local copies, waits for them, and re-layouts: 6.7 us -> none  [per_device(): text_result = jnp.sum(parts * scale[..., None], axis=0) / den[..., None]]
where the time goes in v2:
time: 175 us; the launch traced here: 174 us
  Pallas kernels  164 us (94%)
  local copies, waits for them, and re-layouts  5.59 us (3%)
  other arithmetic  3 us (2%)
    pallas_call x1, Pallas kernels, per_device(): pl.pallas_call(functools.partial(main_kernel, n), out_shape=(jax.ShapeDty...  164 us

profile of v2, /device:TPU:8, one launch (start us, length us, event | category | flops | bytes accessed | tf_op | source)
XLA Modules:
  0.0 174.4 jit_solution(4226347548204816041)
XLA Ops:
  1.3 0.7 fusion.1
  2.0 0.7 fusion.3
  2.7 0.7 select_bitcast_fusion
  3.4 0.1 and_select_fusion.1
  3.6 0.1 and_reduce_fusion
  3.7 0.1 copy.13
  3.8 0.1 broadcast_in_dim.20
  4.0 0.6 broadcast_in_dim.28.own_ref
  4.6 0.6 fusion.tok_ref
  5.2 0.6 pad.5.pick_ref
  5.8 0.8 copy.15.qv_ref
  6.6 164.5 %shard_map.104 = (bf16[256,3072]{1,0:T(8,128)(2,1)}, bf16[16,3072]{1,0:T(8,128)(2,1)}) custom-call(bf16[256,3072]{1,0:T(8,128)(2,1)} %q_ref.1, bf16[256,3072]{1,0:T(8,128)(2,1)} %k_ref.1, bf16[256,3072]{1,0:T(8,128)(2,1)} %v_ref.1, bf16[256,3072]{1,0:T(8,128)(2,1)} %tq_ref.1, bf16[256,3072]{1,0:T(8,128)(2,1)} %tk_ref.1, bf16[256,3072]{1,0:T(8,128)(2,1)} %tv_ref.1, ...), custom_call_target="tpu_custom_call" | custom-call | tf_op jit(solution)/shard_map/pallas_call | solution.py:378
  171.1 0.0 copy-start
  171.1 2.7 %copy.19 = bf16[256,3072]{1,0:T(8,128)(2,1)} copy(bf16[256,3072]{1,0:T(8,128)(2,1)} %get-tuple-element.6) | data formatting | bytes 3145728
  173.8 0.0 copy-done
  173.8 0.6 copy.20
  (7 shorter events, 0.1 us)
Async XLA Ops:
  171.1 2.7 %copy-start = (bf16[16,3072]{1,0:T(8,128)(2,1)S(1)}, bf16[16,3072]{1,0:T(8,128)(2,1)}, u32[]{:S(2)}) copy-start(bf16[16,3072]{1,0:T(8,128)(2,1)} %get-tuple-element.7) | copy-start | bytes 294916

commit v3 on v2

--- a/solution.py
+++ b/solution.py
@@ -206,18 +206,20 @@
             total = jnp.sum(p0 + p1, axis=1, keepdims=True)
             num = None
             for p, value in ((p0, v_ref[:, cols]), (p1, near[pair_slot, 1, c, :, here])):
-                high = p.astype(jnp.bfloat16)
-                low = (p - high.astype(jnp.float32)).astype(jnp.bfloat16)
-                for part in (high, low):
-                    term = jnp.dot(part, value, preferred_element_type=jnp.float32)
+                wide = p * 65537.0
+                high = wide - (wide - p)
+                for part in (high, p - high):
+                    term = jnp.dot(
+                        part.astype(jnp.bfloat16), value, preferred_element_type=jnp.float32
+                    )
                     num = term if num is None else num + term
             num = num.astype(jnp.bfloat16)
             head = j * per_chunk + h
             for b in range(n):
                 rows = slice(b * share, (b + 1) * share)
                 tnum[b, :, to] = num[rows]
-                tstat[b, 0] = jnp.where(lanes == head, top[rows], tstat[b, 0])
-                tstat[b, 1] = jnp.where(lanes == head, total[rows], tstat[b, 1])
+                stat = jnp.where(lanes == head, top[rows], tstat[b])
+                tstat[b] = jnp.where(lanes == head + 64, total[rows], stat)
         return 0
 
     lax.fori_loop(0, text_chunks, text_part, 0)
@@ -316,13 +318,14 @@
     heads = tnum.shape[2] // HD
     for e in range(2):
         top = lax.fori_loop(
-            1, n // 2, lambda i, m: jnp.maximum(m, rstat[2 * i + e, 0]), rstat[e, 0]
+            1, n // 2, lambda i, m: jnp.maximum(m, rstat[2 * i + e]), rstat[e]
         )
 
         def add(i, carry):
             den, nums = carry
-            scale = jnp.exp2((rstat[2 * i + e, 0] - top) * LOG2E_SCALE)
-            den = den + scale * rstat[2 * i + e, 1]
+            stat = rstat[2 * i + e]
+            scale = jnp.exp2((stat - top) * LOG2E_SCALE)
+            den = den + scale * jnp.roll(stat, 64, axis=1)
             nums = tuple(
                 nums[j]
                 + rnum[2 * i + e, :, j * HD:(j + 1) * HD].astype(jnp.float32) * scale[:, j:j + 1]
@@ -388,9 +391,9 @@
             pltpu.VMEM((4, 8, tokens), jnp.float32),
             pltpu.VMEM((2, chunks, tokens, WIDTH), jnp.bfloat16),
             pltpu.VMEM((n, share, width // 2), jnp.bfloat16),
-            pltpu.VMEM((n, 2, share, 128), jnp.float32),
+            pltpu.VMEM((n, share, 128), jnp.float32),
             pltpu.VMEM((n, share, width // 2), jnp.bfloat16),
-            pltpu.VMEM((n, 2, share, 128), jnp.float32),
+            pltpu.VMEM((n, share, 128), jnp.float32),
             dma((4, 2, chunks)),
             dma((4, 2, chunks)),
             dma((4,)),

time: 175 us -> 172 us (0.983)
  Pallas kernels: 164 us -> 162 us
    pallas_call x1, Pallas kernels: 164 us -> 162 us  [per_device(): pl.pallas_call(functools.partial(main_kernel, n), out_shape=(jax.ShapeDty...]
where the time goes in v3:
time: 172 us
  Pallas kernels  162 us (94%)
  local copies, waits for them, and re-layouts  5.59 us (3%)
  other arithmetic  3 us (2%)
    pallas_call x1, Pallas kernels, per_device(): pl.pallas_call(functools.partial(main_kernel, n), out_shape=(jax.ShapeDty...  162 us

profile of v3, /device:TPU:8, one launch (start us, length us, event | category | flops | bytes accessed | tf_op | source)
XLA Modules:
  0.0 171.7 jit_solution(5628569773562264725)
XLA Ops:
  1.3 0.7 fusion.1
  2.0 0.7 fusion.3
  2.7 0.7 select_bitcast_fusion
  3.4 0.1 and_select_fusion.1
  3.6 0.1 and_reduce_fusion
  3.7 0.1 copy.13
  3.8 0.1 broadcast_in_dim.20
  4.0 0.6 broadcast_in_dim.28.own_ref
  4.6 0.6 fusion.tok_ref
  5.2 0.6 pad.5.pick_ref
  5.8 0.8 copy.15.qv_ref
  6.6 161.7 %shard_map.104 = (bf16[256,3072]{1,0:T(8,128)(2,1)}, bf16[16,3072]{1,0:T(8,128)(2,1)}) custom-call(bf16[256,3072]{1,0:T(8,128)(2,1)} %q_ref.1, bf16[256,3072]{1,0:T(8,128)(2,1)} %k_ref.1, bf16[256,3072]{1,0:T(8,128)(2,1)} %v_ref.1, bf16[256,3072]{1,0:T(8,128)(2,1)} %tq_ref.1, bf16[256,3072]{1,0:T(8,128)(2,1)} %tk_ref.1, bf16[256,3072]{1,0:T(8,128)(2,1)} %tv_ref.1, ...), custom_call_target="tpu_custom_call" | custom-call | tf_op jit(solution)/shard_map/pallas_call | solution.py:381
  168.3 0.0 copy-start
  168.3 2.7 %copy.19 = bf16[256,3072]{1,0:T(8,128)(2,1)} copy(bf16[256,3072]{1,0:T(8,128)(2,1)} %get-tuple-element.6) | data formatting | bytes 3145728
  171.0 0.0 copy-done
  171.0 0.6 copy.20
  (7 shorter events, 0.1 us)
Async XLA Ops:
  168.3 2.7 %copy-start = (bf16[16,3072]{1,0:T(8,128)(2,1)S(1)}, bf16[16,3072]{1,0:T(8,128)(2,1)}, u32[]{:S(2)}) copy-start(bf16[16,3072]{1,0:T(8,128)(2,1)} %get-tuple-element.7) | copy-start | bytes 294916

commit v4 on v3

--- a/solution.py
+++ b/solution.py
@@ -213,7 +213,6 @@
                         part.astype(jnp.bfloat16), value, preferred_element_type=jnp.float32
                     )
                     num = term if num is None else num + term
-            num = num.astype(jnp.bfloat16)
             head = j * per_chunk + h
             for b in range(n):
                 rows = slice(b * share, (b + 1) * share)
@@ -390,9 +389,9 @@
             pltpu.VMEM((4, 2, chunks, tokens, WIDTH), jnp.bfloat16),
             pltpu.VMEM((4, 8, tokens), jnp.float32),
             pltpu.VMEM((2, chunks, tokens, WIDTH), jnp.bfloat16),
-            pltpu.VMEM((n, share, width // 2), jnp.bfloat16),
+            pltpu.VMEM((n, share, width // 2), jnp.float32),
             pltpu.VMEM((n, share, 128), jnp.float32),
-            pltpu.VMEM((n, share, width // 2), jnp.bfloat16),
+            pltpu.VMEM((n, share, width // 2), jnp.float32),
             pltpu.VMEM((n, share, 128), jnp.float32),
             dma((4, 2, chunks)),
             dma((4, 2, chunks)),

time: 172 us -> 190 us (1.10)
  Pallas kernels: 162 us -> 179 us
    pallas_call x1, Pallas kernels: 162 us -> 179 us  [per_device(): pl.pallas_call(functools.partial(main_kernel, n), out_shape=(jax.ShapeDty...]
where the time goes in v4:
time: 190 us; the launch traced here: 189 us
  Pallas kernels  179 us (94%)
  local copies, waits for them, and re-layouts  5.59 us (3%)
  other arithmetic  3 us (2%)
    pallas_call x1, Pallas kernels, per_device(): pl.pallas_call(functools.partial(main_kernel, n), out_shape=(jax.ShapeDty...  179 us

profile of v4, /device:TPU:8, one launch (start us, length us, event | category | flops | bytes accessed | tf_op | source)
XLA Modules:
  0.0 188.6 jit_solution(1532515651351826223)
XLA Ops:
  1.3 0.7 fusion.1
  2.0 0.7 fusion.3
  2.7 0.7 select_bitcast_fusion
  3.4 0.1 and_select_fusion.1
  3.6 0.1 and_reduce_fusion
  3.7 0.1 copy.13
  3.8 0.1 broadcast_in_dim.20
  4.0 0.6 broadcast_in_dim.28.own_ref
  4.6 0.6 fusion.tok_ref
  5.2 0.6 pad.5.pick_ref
  5.8 0.8 copy.15.qv_ref
  6.6 178.7 %shard_map.104 = (bf16[256,3072]{1,0:T(8,128)(2,1)}, bf16[16,3072]{1,0:T(8,128)(2,1)}) custom-call(bf16[256,3072]{1,0:T(8,128)(2,1)} %q_ref.1, bf16[256,3072]{1,0:T(8,128)(2,1)} %k_ref.1, bf16[256,3072]{1,0:T(8,128)(2,1)} %v_ref.1, bf16[256,3072]{1,0:T(8,128)(2,1)} %tq_ref.1, bf16[256,3072]{1,0:T(8,128)(2,1)} %tk_ref.1, bf16[256,3072]{1,0:T(8,128)(2,1)} %tv_ref.1, ...), custom_call_target="tpu_custom_call" | custom-call | tf_op jit(solution)/shard_map/pallas_call | solution.py:380
  185.3 0.0 copy-start
  185.3 2.7 %copy.19 = bf16[256,3072]{1,0:T(8,128)(2,1)} copy(bf16[256,3072]{1,0:T(8,128)(2,1)} %get-tuple-element.6) | data formatting | bytes 3145728
  188.0 0.0 copy-done
  188.0 0.6 copy.20
  (7 shorter events, 0.1 us)
Async XLA Ops:
  185.3 2.7 %copy-start = (bf16[16,3072]{1,0:T(8,128)(2,1)S(1)}, bf16[16,3072]{1,0:T(8,128)(2,1)}, u32[]{:S(2)}) copy-start(bf16[16,3072]{1,0:T(8,128)(2,1)} %get-tuple-element.7) | copy-start | bytes 294916
